TPU v7x, 128 devices: a whole 4x4x4 slice. The times are simulated.
128 devices in a mesh: dp: 64 (over x_lo, y, z, core), expert: 2 (over x_hi).
Axes of the slice: x: 4 (x_hi: 2, x_lo: 2; x = x_hi * 2 + x_lo), y: 4, z: 4, core: 2. Of those that a mesh axis runs over, the one named last changes fastest.
Arguments:
- tokens: bfloat16 [131072, 3584], P(('dp', 'expert')), may hold values from -6 to 6
- assignment: int32 [131072, 1], P(('dp', 'expert')), may hold values from 0 to 1; in each aligned block of 1024 rows (0 to 1023, 1024 to 2047, ...) at most 640 rows name the same one
- gate: bfloat16 [131072], P(('dp', 'expert')), may hold values from 0.099609375 to 1
- weight: bfloat16 [2, 3584, 1024], P('expert', 'dp'), may hold values from -0.09375 to 0.09375
- cotangent: bfloat16 [2, 81920, 1024], P('expert', 'dp'), may hold values from -6 to 6
Outputs:
- activated: bfloat16 [2, 81920, 1024], P('expert', 'dp')
- grad_tokens: bfloat16 [131072, 3584], P(('dp', 'expert'))
- grad_gate: bfloat16 [131072], P(('dp', 'expert'))
- grad_weight: float32 [2, 3584, 1024], P('expert', 'dp')
Inputs may be any that keep to these rules, and one draw needn't show every extreme that they name: `assignment`: of the tokens of one device at most 640 name the same expert, and in some device exactly 640 do.
All inputs are finite; a program needn't handle non-finite values.
Results may differ from a plain program's by a relative error of at most 0.0049.
Values may be sent and summed in bfloat16 or wider, within the bound.
A program may use at most 128 MiB of HBM per device.

v0:
```python
import jax
import jax.numpy as jnp
from jax import lax
from jax.experimental import pallas as pl
from jax.experimental.pallas import tpu as pltpu
from jax.sharding import PartitionSpec as P

CAP = 640
TOK = 1024
D = 3584
F = 1024
HALF = 512
ROWS = 112
PLANE = 1792
BLK = 512
NBLK = D // BLK
EARLY = 3
MESH = pl.DeviceIdType.MESH
F32 = jnp.float32
BF16 = jnp.bfloat16


def place():
    d, e = lax.axis_index("dp"), lax.axis_index("expert")
    core, z, y, x_lo = d % 2, (d // 2) % 4, (d // 8) % 4, d // 32
    a = y + core * (z - y)
    b = z + core * (y - z)
    return e, x_lo, a, b, core


def device(x, a, b, core):
    x, a, b = x % 4, a % 4, b % 4
    y = a + core * (b - a)
    z = b + core * (a - b)
    return (((x % 2) * 4 + y) * 4 + z) * 2 + core, x // 2


def chunk_row(a, b, core):
    a, b = a % 4, b % 4
    y = a + core * (b - a)
    z = b + core * (a - b)
    return (y * 4 + z) * ROWS


def rows_at(start, size, by=16):
    return pl.ds(pl.multiple_of(start, by), size)


def copy_to(src, dst, send_sem, recv_sem, to):
    return pltpu.make_async_remote_copy(
        src_ref=src, dst_ref=dst, send_sem=send_sem, recv_sem=recv_sem, device_id=to, device_id_type=MESH
    )


def send(*args):
    copy_to(*args).start()


def arrived(ref, sem):
    pltpu.make_async_copy(ref, ref, sem).wait()


def nn(p, q):
    return jnp.dot(p, q, preferred_element_type=F32)


def nt(p, q):
    return lax.dot_general(p, q, (((1,), (1,)), ((), ())), preferred_element_type=F32)


def tn(p, q):
    return lax.dot_general(p, q, (((0,), (0,)), ((), ())), preferred_element_type=F32)


def loop(first, last, f):
    def one(i, carry):
        f(i)
        return carry

    lax.fori_loop(first, last, one, 0)


def one_hot_rows(owner_ref, Q):
    owner = jnp.broadcast_to(owner_ref[...], (8, TOK)).astype(F32)
    upper = (
        lax.broadcasted_iota(jnp.int32, (TOK, TOK), 0) <= lax.broadcasted_iota(jnp.int32, (TOK, TOK), 1)
    ).astype(BF16)
    ones = nn(owner.astype(BF16), upper)
    token = lax.broadcasted_iota(jnp.int32, (8, TOK), 1).astype(F32)
    slot = jnp.where(owner > 0.5, CAP + ones - 1.0, token - ones)[:1].astype(jnp.int32)

    def some(i):
        rows = lax.broadcasted_iota(jnp.int32, (64, TOK), 0) + i * 64
        Q[rows_at(i * 64, 64), :] = (rows == slot).astype(F32).astype(BF16)

    loop(0, 2 * CAP // 64, some)


def main_kernel(
    w_ref, owner_ref, gate_ref, x_hbm, cot_hbm,
    act_out, tok_out, sg_out, gate_out, wg_out,
    W, XS, Q, pre, PG, ACT, ggs, gs,
    SB, RSB, OWN, S, RB, T2, KB, SA, RA, SX, RX, KA, MINE, FIN, SG,
    s_loc, s_blk, s_first, r_first, s_x, r_x, s_a, r_a, s_b, r_b, s_sib, r_sib, s_cot, r_cot,
    s_sb, r_sb, credit, s_ra, r_ra, s_rb, r_rb, s_rx, r_rx, s_fin, r_fin, s_act, r_act, s_sg, s_tok,
):
    e, xl, a, b, core = place()
    x = 2 * e + xl
    sib = device(x, b, a, 1 - core)
    half = pl.ds(pl.multiple_of(core * HALF, HALF), HALF)
    other = pl.ds(pl.multiple_of((1 - core) * HALF, HALF), HALF)

    def plane(j):
        ee = e + (j // 2) * (1 - 2 * e)
        flip = ((j + 1) // 2) % 2
        return ee, xl + flip * (1 - 2 * xl)

    def target(j):
        return plane(j + 1 - 2 * (j % 2))

    def away(p):
        return (2 * p[0] + p[1] - x + 4) % 4

    def block_cols(c):
        return pl.ds(pl.multiple_of(c * BLK, BLK), BLK)

    def block_of(i):
        return (i + 3 * xl) % NBLK

    def load_x(i):
        return pltpu.make_async_copy(x_hbm.at[:, block_cols(block_of(i))], SG.at[i % 2, :TOK], s_blk.at[i % 2])

    load_x(0).start()
    load_x(1).start()
    load_cot = pltpu.make_async_copy(cot_hbm.at[0, rows_at(e * CAP, CAP), :], PG.at[e], s_loc.at[0])
    load_cot.start()

    barrier = pltpu.get_barrier_semaphore()
    peers = [sib]
    for o in (1, 2, 3):
        peers.append(device(x + o, a, b, core))
    for o in (1, 3):
        peers += [device(x, a + o, b, core), device(x, a, b + o, core)]
    for peer in peers:
        pl.semaphore_signal(barrier, inc=1, device_id=peer, device_id_type=MESH)
    pl.semaphore_wait(barrier, len(peers))

    left, right = w_ref[0, :, :HALF].astype(F32), w_ref[0, :, HALF:].astype(F32)
    FIN[1, :56] = jnp.where(core == 0, right, left)
    swap = copy_to(FIN.at[1, :56], FIN.at[0, rows_at(core * 56, 56, 8), :], s_first.at[0], r_first.at[0], sib)
    swap.start()
    FIN[0, rows_at(core * 56, 56, 8), :] = jnp.where(core == 0, left, right)
    swap.wait()

    def piece(j, r, o):
        ee, ll = plane(j)
        return W.at[ee, rows_at(ll * PLANE + chunk_row(a + r, b + o, core), ROWS), half]

    def to_sibling(j, ref):
        send(ref, ref, s_sib.at[j], r_sib.at[j], sib)

    mine = piece(0, 0, 0)
    W[e, rows_at(xl * PLANE + chunk_row(a, b, core), ROWS), half] = FIN[0].astype(BF16)

    def send_a(j):
        ref = piece(j, 0, 0)
        for s in (1, 3):
            send(ref, ref, s_a.at[j, s - 1], r_a.at[j, 3 - s], device(x, a + s, b, core))
        to_sibling(j, ref)

    def take_a(j):
        for o in (1, 3):
            arrived(piece(j, o, 0), r_a.at[j, o - 1])
            to_sibling(j, piece(j, o, 0))
        o = 3 - 2 * (j % 2)
        ref = piece(j, o, 0)
        send(ref, ref, s_a.at[j, 1], r_a.at[j, 1], device(x, a - o, b, core))

    def far_a(j):
        arrived(piece(j, 2, 0), r_a.at[j, 1])
        to_sibling(j, piece(j, 2, 0))

    def send_b(j, r):
        ref = piece(j, r, 0)
        for s in (1, 3):
            send(ref, ref, s_b.at[j, s - 1, r], r_b.at[j, 3 - s, r], device(x, a, b + s, core))

    def take_b(j, r):
        for o in (1, 3):
            arrived(piece(j, r, o), r_b.at[j, o - 1, r])
            to_sibling(j, piece(j, r, o))
        o = 3 if r < 2 else 1
        ref = piece(j, r, o)
        send(ref, ref, s_b.at[j, 1, r], r_b.at[j, 1, r], device(x, a, b - o, core))

    def far_b(j, r):
        arrived(piece(j, r, 2), r_b.at[j, 1, r])
        to_sibling(j, piece(j, r, 2))

    for s in (1, 3, 2):
        send(mine, mine, s_x.at[s - 1], r_x.at[3 - s], device(x + s, a, b, core))
    send_a(0)
    send_b(0, 0)

    one_hot_rows(owner_ref, Q)
    g8 = gate_ref[...].astype(F32)
    gate_row = jnp.concatenate([g8[i : i + 1] for i in range(8)], axis=1)
    gs[...] = nt(Q[...], jnp.broadcast_to(gate_row, (128, TOK)).astype(BF16))

    take_a(0)
    send_b(0, 1)
    send_b(0, 3)
    partner = device(x + 2, a, b, core)
    theirs_rows = rows_at((1 - e) * CAP, CAP)
    send(cot_hbm.at[0, theirs_rows, :], PG.at[e], s_cot.at[0], r_cot.at[0], partner)
    for j in (1, 2, 3):
        arrived(piece(j, 0, 0), r_x.at[away(plane(j)) - 1])
        send_a(j)
    far_a(0)
    send_b(0, 2)

    def dispatch(i):
        load_x(i).wait()
        cols = block_cols(block_of(i))
        XS[:, cols] = nn(Q[...], SG[i % 2, :TOK]).astype(BF16)

        @pl.when(i < NBLK - 2)
        def _():
            load_x(i + 2).start()

    def slots_of(k, l):
        return XS[rows_at(k * CAP, CAP), pl.ds(pl.multiple_of(l * PLANE, 256), PLANE)]

    def forward(j, h):
        ee, ll = plane(j)
        cols = slice(h * HALF, (h + 1) * HALF)
        part = nn(slots_of(ee, ll), W[ee, rows_at(ll * PLANE, PLANE, 256), cols])
        pre[:, cols] = jnp.where(j % 2 == 0, part, pre[:, cols] + part)

    def pointwise(k):
        def tile(i):
            rows = rows_at(i * 64, 64, 64)
            gate = gs[rows_at(k * CAP + i * 64, 64, 64), :]
            gate = jnp.concatenate([gate] * 4, axis=1)
            total = jnp.zeros((64, 1), F32)
            for h in (0, 1):
                cols = slice(h * HALF, (h + 1) * HALF)
                z = pre[rows, cols]
                s = 0.5 + 0.5 * jnp.tanh(0.5 * z)
                shaped = z * s
                up = PG[k, rows, cols].astype(F32)
                ACT[rows, cols] = (gate * shaped).astype(BF16)
                total += jnp.sum(up * shaped, axis=1, keepdims=True)
                PG[k, rows, cols] = (up * gate * (s * (1.0 + z * (1.0 - s)))).astype(BF16)
            ggs[rows_at(k * CAP + i * 64, 64, 64), :] = jnp.broadcast_to(total, (64, 128))

        loop(0, CAP // 64, tile)

    def theirs(j):
        ee, ll = target(j)
        for i in (0, 1):
            part = XS[rows_at(ee * CAP, CAP), pl.ds(pl.multiple_of(ll * PLANE + i * 896, 128), 896)]
            SB[i * 896 : (i + 1) * 896, :] = tn(part, PG[ee, :, other]).astype(BF16)
        send(SB, RSB.at[j % 2], s_sb.at[0], r_sb.at[j % 2], sib)

    def ours(j):
        ee, ll = target(j)
        for i in (0, 1):
            part = XS[rows_at(ee * CAP, CAP), pl.ds(pl.multiple_of(ll * PLANE + i * 896, 128), 896)]
            OWN[i * 896 : (i + 1) * 896, :] = tn(part, PG[ee, :, half])

    def first_sends(j):
        arrived(RSB.at[j % 2], r_sb.at[j % 2])

        def summed(r, o):
            rows = rows_at(chunk_row(a + r, b + o, core), ROWS)
            return rows, OWN[rows, :] + RSB[j % 2, rows, :].astype(F32)

        for r in (0, 2, 1, 3):
            S[j % 2, 1, r] = summed(r, 2)[1].astype(BF16)
            s = 1 if r < 2 else 3
            send(S.at[j % 2, 1, r], T2.at[j, r], s_rb.at[j, 1, r], r_rb.at[j, 1, r], device(x, a, b + s, core))
        for r in (2, 0, 3, 1):
            s = 3 if r < 2 else 1
            S[j % 2, s - 1, r] = summed(r, s)[1].astype(BF16)
            send(
                S.at[j % 2, s - 1, r], RB.at[j, s // 2, r],
                s_rb.at[j, s - 1, r], r_rb.at[j, 3 - s, r], device(x, a, b + s, core),
            )
        for r in (0, 1, 2, 3):
            KB[j % 2, r] = summed(r, 0)[1]
            rows, total = summed(r, 1 if r < 2 else 3)
            OWN[rows, :] = total

    def relayed_sends(j):
        for r in (0, 2, 1, 3):
            s = 1 if r < 2 else 3
            arrived(T2.at[j, r], r_rb.at[j, 1, r])
            rows = rows_at(chunk_row(a + r, b + s, core), ROWS)
            S[j % 2, s - 1, r] = (OWN[rows, :] + T2[j, r].astype(F32)).astype(BF16)
            send(
                S.at[j % 2, s - 1, r], RB.at[j, s // 2, r],
                s_rb.at[j, s - 1, r], r_rb.at[j, 3 - s, r], device(x, a, b + s, core),
            )

    def sent_b(j):
        for o in (0, 1, 2):
            for r in (0, 1, 2, 3):
                arrived(S.at[j % 2, o, r], s_rb.at[j, o, r])

    def sent_a(j):
        for s in (0, 1, 2):
            arrived(SA.at[j % 2, s], s_ra.at[j, s])

    def finish_b(j):
        def total(r):
            for o in (1, 3):
                arrived(RB.at[j, 1 if o == 3 else 0, r], r_rb.at[j, o - 1, r])
            return KB[j % 2, r] + RB[j, 0, r].astype(F32) + RB[j, 1, r].astype(F32)

        @pl.when(j >= 2)
        def _():
            sent_a(j - 2)

        s = 1 + 2 * (j % 2)
        SA[j % 2, 1] = total(2).astype(BF16)
        send(SA.at[j % 2, 1], RA.at[j, 1], s_ra.at[j, 1], r_ra.at[j, 1], device(x, a + s, b, core))
        for r in (1, 3, 0):
            KB[j % 2, r] = total(r)
        t = 4 - s
        SA[j % 2, t - 1] = KB[j % 2, t].astype(BF16)
        send(SA.at[j % 2, t - 1], RA.at[j, 3 - t], s_ra.at[j, t - 1], r_ra.at[j, 3 - t], device(x, a + t, b, core))

    def relay_a(j):
        s = 1 + 2 * (j % 2)
        arrived(RA.at[j, 1], r_ra.at[j, 1])
        SA[j % 2, s - 1] = (KB[j % 2, s] + RA[j, 1].astype(F32)).astype(BF16)
        send(SA.at[j % 2, s - 1], RA.at[j, 3 - s], s_ra.at[j, s - 1], r_ra.at[j, 3 - s], device(x, a + s, b, core))
        KA[j % 2] = KB[j % 2, 0]

    def finish_a(j):
        total = KA[j % 2]
        for o in (1, 3):
            arrived(RA.at[j, o - 1], r_ra.at[j, o - 1])
            total += RA[j, o - 1].astype(F32)
        return total

    def finish_x(j):
        o = away(target(j))
        SX[o - 1] = finish_a(j).astype(BF16)
        send(SX.at[o - 1], RX.at[3 - o], s_rx.at[o - 1], r_rx.at[3 - o], device(x + o, a, b, core))

    def slot_grad(k, c):
        cols = block_cols(c)

        @pl.when(c >= 2)
        def _():
            arrived(SG.at[c % 2, :CAP], s_sg.at[c % 2])

        SG[c % 2, :CAP] = nt(PG[k], W[k, cols, :]).astype(BF16)
        pltpu.make_async_copy(SG.at[c % 2, :CAP], sg_out.at[k, :, cols], s_sg.at[c % 2]).start()

    def slot_grads(k, first, last):
        loop(first, last, lambda c: slot_grad(k, c))

    def drain_sg():
        for i in (0, 1):
            arrived(SG.at[i, :CAP], s_sg.at[i])

    def gather_step(j):
        for i, r in enumerate((0, 1, 3, 2)):

            @pl.when(j == 0)
            def _():
                dispatch(i)

            if i == 0:

                @pl.when(j > 0)
                def _():
                    forward(j - 1, 0)

            if i == 1:

                @pl.when(j > 0)
                def _():
                    forward(j - 1, 1)

            if i == 2:

                @pl.when(j == 1)
                def _():
                    dispatch(4)
                    dispatch(5)

                @pl.when(j == 2)
                def _():
                    load_cot.wait()
                    pointwise(e)

            if i == 3:

                @pl.when(j == 1)
                def _():
                    dispatch(6)

                @pl.when(j == 2)
                def _():
                    theirs(0)

            take_b(j, r)

        @pl.when(j < 3)
        def _():
            send_b(j + 1, 0)
            take_a(j + 1)
            send_b(j + 1, 1)
            send_b(j + 1, 3)
            far_a(j + 1)
            send_b(j + 1, 2)

        @pl.when(j == 2)
        def _():
            ours(0)
            pltpu.make_async_copy(ACT, act_out.at[0, rows_at(e * CAP, CAP), :], s_loc.at[1]).start()

        @pl.when(j == 3)
        def _():
            first_sends(0)
            pl.semaphore_signal(credit, inc=1, device_id=sib, device_id_type=MESH)
            slot_grads(e, 0, 4)

        for r in (0, 1, 3, 2):
            far_b(j, r)

        @pl.when(j == 3)
        def _():
            slot_grads(e, 4, NBLK)

        ee, ll = plane(j)
        arrived(W.at[ee, rows_at(ll * PLANE, PLANE), other], r_sib.at[j])

    loop(0, 4, gather_step)
    drain_sg()

    def reduce_step(j):
        @pl.when(j > 0)
        def _():
            @pl.when(j >= 2)
            def _():
                relay_a(j - 2)
                sent_b(j - 2)

            first_sends(j)

            @pl.when(j == 1)
            def _():
                pl.semaphore_signal(credit, inc=1, device_id=sib, device_id_type=MESH)
                arrived(PG.at[1 - e], r_cot.at[0])
                arrived(ACT, s_loc.at[1])
                pointwise(1 - e)
                send(ACT, act_out.at[0, rows_at(e * CAP, CAP), :], s_act.at[0], r_act.at[0], partner)

        @pl.when(j < 3)
        def _():
            arrived(SB, s_sb.at[0])

            @pl.when(j >= 1)
            def _():
                pl.semaphore_wait(credit, 1)

            theirs(j + 1)

        @pl.when(j == 0)
        def _():
            forward(3, 0)

        @pl.when(j == 2)
        def _():
            slot_grads(1 - e, 0, 3)

        relayed_sends(j)

        @pl.when(j < 3)
        def _():
            ours(j + 1)

        @pl.when(j == 0)
        def _():
            forward(3, 1)

        @pl.when(j >= 1)
        def _():
            finish_b(j - 1)

        @pl.when(j == 3)
        def _():
            finish_x(0)

    loop(0, 4, reduce_step)
    slot_grads(1 - e, 3, 6)
    relay_a(2)
    MINE[...] = finish_a(1)
    slot_grads(1 - e, 6, NBLK)
    drain_sg()
    finish_b(3)
    finish_x(2)

    def early(c):
        for k in (0, 1):
            pltpu.make_async_copy(
                sg_out.at[k, :, block_cols(c)], SG.at[c % 2, k * CAP : (k + 1) * CAP], s_sg.at[c % 2]
            ).start()

    def combine(c):
        arrived(SG.at[c % 2], s_sg.at[c % 2])

        @pl.when(c >= 2)
        def _():
            arrived(RSB.at[c % 2, :TOK], s_tok.at[c % 2])

        RSB[c % 2, :TOK] = tn(Q[...], SG[c % 2]).astype(BF16)
        pltpu.make_async_copy(RSB.at[c % 2, :TOK], tok_out.at[:, block_cols(c)], s_tok.at[c % 2]).start()

        @pl.when(c + 2 < EARLY)
        def _():
            early(c + 2)

    early(0)
    early(1)
    combine(0)
    relay_a(3)
    loop(1, EARLY, combine)
    gg = ggs[...].T[:8].astype(BF16)
    row = nn(gg, Q[...])
    gate_out[...] = jnp.concatenate([row[:1, i * 128 : (i + 1) * 128] for i in range(8)], axis=0)
    finish_x(3)
    total = MINE[...]
    for o in (1, 2, 3):
        arrived(RX.at[o - 1], r_rx.at[o - 1])
        total += RX[o - 1].astype(F32)
    FIN[0] = total
    away_rows = rows_at((1 - core) * 56, 56, 8)
    kept_rows = rows_at(core * 56, 56, 8)
    last = copy_to(FIN.at[0, away_rows, :], FIN.at[1, away_rows, :], s_fin.at[0], r_fin.at[0], sib)
    last.start()
    last.wait_send()
    arrived(FIN.at[1, kept_rows, :], r_fin.at[0])
    kept, came = FIN[0, kept_rows, :], FIN[1, kept_rows, :]
    wg_out[0, :, :HALF] = jnp.where(core == 0, kept, came)
    wg_out[0, :, HALF:] = jnp.where(core == 0, came, kept)

    for s in (0, 1, 2):
        arrived(mine, s_x.at[s])
        arrived(SX.at[s], s_rx.at[s])
    arrived(cot_hbm.at[0, theirs_rows, :], s_cot.at[0])
    arrived(ACT, s_act.at[0])
    arrived(SB, s_sb.at[0])
    arrived(act_out.at[0, theirs_rows, :], r_act.at[0])
    for i in (0, 1):
        arrived(RSB.at[i, :TOK], s_tok.at[i])

    def drain(j):
        for s in (0, 1, 2):
            arrived(piece(j, 0, 0), s_a.at[j, s])
            for r in (0, 1, 2, 3):
                arrived(piece(j, 0, 0), s_b.at[j, s, r])
        ee, ll = plane(j)
        arrived(W.at[ee, rows_at(ll * PLANE, PLANE), half], s_sib.at[j])

        @pl.when(j >= 2)
        def _():
            sent_a(j)
            sent_b(j)

    loop(0, 4, drain)


def combine_kernel(
    owner_ref, gate_ref, sg_hbm, tok_hbm, act_hbm, wg_hbm,
    gate_out, tok_out, act_out, wg_out,
    Q, SG, TB, TV, AV, GV, s_sg, s_tok, s_in, s_out,
):
    def cols(c):
        return pl.ds(pl.multiple_of(c * BLK, BLK), BLK)

    def load(c):
        return [
            pltpu.make_async_copy(
                sg_hbm.at[k, :, cols(c)], SG.at[c % 2, k * CAP : (k + 1) * CAP], s_sg.at[c % 2, k]
            )
            for k in (0, 1)
        ]

    moves = [
        (act_hbm, AV, act_out),
        (tok_hbm, TV, tok_out.at[:, : EARLY * BLK]),
        (wg_hbm, GV, wg_out),
    ]
    moves = [
        (pltpu.make_async_copy(p, v, s_in.at[i]), pltpu.make_async_copy(v, q, s_out.at[i]))
        for i, (p, v, q) in enumerate(moves)
    ]
    for c in (EARLY, EARLY + 1):
        for k in load(c):
            k.start()
    for k, _ in moves:
        k.start()
    one_hot_rows(owner_ref, Q)
    gate_out[...] = gate_ref[...].astype(BF16)

    def combine(c):
        for k in load(c):
            k.wait()

        @pl.when(c >= EARLY + 2)
        def _():
            arrived(TB.at[c % 2], s_tok.at[c % 2])

        TB[c % 2] = tn(Q[...], SG[c % 2]).astype(BF16)
        pltpu.make_async_copy(TB.at[c % 2], tok_out.at[:, cols(c)], s_tok.at[c % 2]).start()

        @pl.when(c + 2 < NBLK)
        def _():
            for k in load(c + 2):
                k.start()

    loop(EARLY, EARLY + 1, combine)
    for k, m in moves:
        k.wait()
        m.start()
    loop(EARLY + 1, NBLK, combine)
    for i in (0, 1):
        arrived(TB.at[i], s_tok.at[i])
    for _, m in moves:
        m.wait()


def body(tokens, assignment, gate, weight, cotangent):
    ANY, VMEM = pl.BlockSpec(memory_space=pl.ANY), pl.BlockSpec(memory_space=pltpu.VMEM)
    DMA = pltpu.SemaphoreType.DMA
    shape = jax.ShapeDtypeStruct
    owner = assignment.reshape(1, TOK)
    act, tok, sg, grad_gate, grad_weight = pl.pallas_call(
        main_kernel,
        out_shape=(
            shape((1, 2 * CAP, F), BF16),
            shape((TOK, EARLY * BLK), BF16),
            shape((2, CAP, D), BF16),
            shape((8, 128), F32),
            shape((1, 56, F), F32),
        ),
        in_specs=[VMEM, VMEM, VMEM, ANY, ANY],
        out_specs=(ANY, ANY, ANY, VMEM, VMEM),
        scratch_shapes=[
            pltpu.VMEM((2, D, F), BF16),
            pltpu.VMEM((2 * CAP, D), BF16),
            pltpu.VMEM((2 * CAP, TOK), BF16),
            pltpu.VMEM((CAP, F), F32),
            pltpu.VMEM((2, CAP, F), BF16),
            pltpu.VMEM((CAP, F), BF16),
            pltpu.VMEM((2 * CAP, 128), F32),
            pltpu.VMEM((2 * CAP, 128), F32),
            pltpu.VMEM((PLANE, HALF), BF16),
            pltpu.VMEM((2, PLANE, HALF), BF16),
            pltpu.VMEM((PLANE, HALF), F32),
            pltpu.VMEM((2, 3, 4, ROWS, HALF), BF16),
            pltpu.VMEM((4, 2, 4, ROWS, HALF), BF16),
            pltpu.VMEM((4, 4, ROWS, HALF), BF16),
            pltpu.VMEM((2, 4, ROWS, HALF), F32),
            pltpu.VMEM((2, 3, ROWS, HALF), BF16),
            pltpu.VMEM((4, 3, ROWS, HALF), BF16),
            pltpu.VMEM((3, ROWS, HALF), BF16),
            pltpu.VMEM((3, ROWS, HALF), BF16),
            pltpu.VMEM((2, ROWS, HALF), F32),
            pltpu.VMEM((ROWS, HALF), F32),
            pltpu.VMEM((2, ROWS, HALF), F32),
            pltpu.VMEM((2, 2 * CAP, BLK), BF16),
            DMA((2,)), DMA((2,)), DMA((1,)), DMA((1,)), DMA((3,)), DMA((3,)), DMA((4, 3)), DMA((4, 3)),
            DMA((4, 3, 4)), DMA((4, 3, 4)), DMA((4,)), DMA((4,)), DMA((1,)), DMA((1,)),
            DMA((1,)), DMA((2,)), pltpu.SemaphoreType.REGULAR, DMA((4, 3)), DMA((4, 3)),
            DMA((4, 3, 4)), DMA((4, 3, 4)), DMA((3,)), DMA((3,)), DMA((1,)), DMA((1,)), DMA((1,)), DMA((1,)),
            DMA((2,)), DMA((2,)),
        ],
        compiler_params=pltpu.CompilerParams(collective_id=1, has_side_effects=True, vmem_limit_bytes=61 * 2**20),
        name="gather_and_reduce",
    )(weight, owner, gate.reshape(8, 128), tokens, cotangent)
    grad_gate, grad_tokens, activated, grad_weight = pl.pallas_call(
        combine_kernel,
        out_shape=(
            shape((8, 128), BF16),
            shape((TOK, D), BF16),
            shape((1, 2 * CAP, F), BF16),
            shape((1, 56, F), F32),
        ),
        in_specs=[VMEM, VMEM, ANY, ANY, ANY, ANY],
        out_specs=(VMEM, ANY, ANY, ANY),
        scratch_shapes=[
            pltpu.VMEM((2 * CAP, TOK), BF16),
            pltpu.VMEM((2, 2 * CAP, BLK), BF16),
            pltpu.VMEM((2, TOK, BLK), BF16),
            pltpu.VMEM((TOK, EARLY * BLK), BF16),
            pltpu.VMEM((1, 2 * CAP, F), BF16),
            pltpu.VMEM((1, 56, F), F32),
            DMA((2, 2)), DMA((2,)), DMA((3,)), DMA((3,)),
        ],
        compiler_params=pltpu.CompilerParams(vmem_limit_bytes=60 * 2**20),
        name="combine_tokens",
    )(owner, grad_gate, sg, tok, act, grad_weight)
    return activated, grad_tokens, grad_gate.reshape(TOK), grad_weight


def solution(mesh):
    placed = (
        P(("dp", "expert"), None),
        P(("dp", "expert"), None),
        P(("dp", "expert")),
        P("expert", "dp", None),
        P("expert", "dp", None),
    )
    return jax.shard_map(
        body,
        mesh=mesh,
        in_specs=placed,
        out_specs=(
            P("expert", "dp", None),
            P(("dp", "expert"), None),
            P(("dp", "expert")),
            P("expert", "dp", None),
        ),
        check_vma=False,
    )
```

profile of v0, /device:TPU:1, one launch (start us, length us, event | category | flops | bytes accessed | tf_op | source)
XLA Modules:
  0.0 144.2 jit_solution(4129557141960869776)
XLA Ops:
  0.6 132.8 %gather_and_reduce.1 = (bf16[1,1280,1024]{2,1,0:T(8,128)(2,1)}, bf16[1024,1536]{1,0:T(8,128)(2,1)}, bf16[2,640,3584]{2,1,0:T(8,128)(2,1)}, f32[8,128]{1,0:T(8,128)}, f32[1,56,1024]{2,1,0:T(8,128)}) custom-call(bf16[1,56,1024]{2,1,0:T(8,128)(2,1)} %w_ref.1, s32[1,1024]{1,0:T(1,128)} %bitcast.3, bf16[8,128]{1,0:T(8,128)(2,1)} %bitcast.5, ...), custom_call_target="tpu_custom_call" | custom-call | tf_op jit(solution)/shard_map/gather_and_reduce/pallas_call | solution.py:644
  133.4 10.7 %combine_tokens.1 = (bf16[8,128]{1,0:T(8,128)(2,1)}, bf16[1024,3584]{1,0:T(8,128)(2,1)}, bf16[1,1280,1024]{2,1,0:T(8,128)(2,1)}, f32[1,56,1024]{2,1,0:T(8,128)}) custom-call(s32[1,1024]{1,0:T(1,128)} %bitcast.4, f32[8,128]{1,0:T(8,128)} %get-tuple-element.13.gate_ref, bf16[2,640,3584]{2,1,0:T(8,128)(2,1)} %get-tuple-element.14.sg_hbm, ...), custom_call_target="tpu_custom_call" | custom-call | tf_op jit(solution)/shard_map/combine_tokens/pallas_call | solution.py:688
where the time goes:
time: 144 us
  Pallas kernels  143 us (99%)
    pallas_call x1, Pallas kernels, body(): pl.pallas_call(main_kernel, out_shape=(shape((1, 2 * CAP, F), BF16), shap...  133 us
    pallas_call x1, Pallas kernels, body(): pl.pallas_call(combine_kernel, out_shape=(shape((8, 128), BF16), shape((T...  10.7 us

commit v1 on v0

v1 whole, which is shorter than its diff:
```python
import jax
import jax.numpy as jnp
from jax import lax
from jax.experimental import pallas as pl
from jax.experimental.pallas import tpu as pltpu
from jax.sharding import PartitionSpec as P

CAP = 640
TOK = 1024
D = 3584
F = 1024
HALF = 512
ROWS = 112
PLANE = 1792
BLK = 512
NBLK = D // BLK
EARLY = 3
MESH = pl.DeviceIdType.MESH
F32 = jnp.float32
BF16 = jnp.bfloat16


def place():
    d, e = lax.axis_index("dp"), lax.axis_index("expert")
    core, z, y, x_lo = d % 2, (d // 2) % 4, (d // 8) % 4, d // 32
    a = y + core * (z - y)
    b = z + core * (y - z)
    return e, x_lo, a, b, core


def device(x, a, b, core):
    x, a, b = x % 4, a % 4, b % 4
    y = a + core * (b - a)
    z = b + core * (a - b)
    return (((x % 2) * 4 + y) * 4 + z) * 2 + core, x // 2


def rows_at(start, size, by=16):
    return pl.ds(pl.multiple_of(start, by), size)


def copy_to(src, dst, send_sem, recv_sem, to):
    return pltpu.make_async_remote_copy(
        src_ref=src, dst_ref=dst, send_sem=send_sem, recv_sem=recv_sem, device_id=to, device_id_type=MESH
    )


def send(*args):
    copy_to(*args).start()


def arrived(ref, sem):
    pltpu.make_async_copy(ref, ref, sem).wait()


def nn(p, q):
    return jnp.dot(p, q, preferred_element_type=F32)


def nt(p, q):
    return lax.dot_general(p, q, (((1,), (1,)), ((), ())), preferred_element_type=F32)


def tn(p, q):
    return lax.dot_general(p, q, (((0,), (0,)), ((), ())), preferred_element_type=F32)


def loop(first, last, f):
    def one(i, carry):
        f(i)
        return carry

    lax.fori_loop(first, last, one, 0)


def one_hot_rows(owner_ref, Q):
    owner = jnp.broadcast_to(owner_ref[...], (8, TOK)).astype(F32)
    upper = (
        lax.broadcasted_iota(jnp.int32, (TOK, TOK), 0) <= lax.broadcasted_iota(jnp.int32, (TOK, TOK), 1)
    ).astype(BF16)
    ones = nn(owner.astype(BF16), upper)
    token = lax.broadcasted_iota(jnp.int32, (8, TOK), 1).astype(F32)
    slot = jnp.where(owner > 0.5, CAP + ones - 1.0, token - ones)[:1].astype(jnp.int32)

    def some(i):
        rows = lax.broadcasted_iota(jnp.int32, (64, TOK), 0) + i * 64
        Q[rows_at(i * 64, 64), :] = (rows == slot).astype(F32).astype(BF16)

    loop(0, 2 * CAP // 64, some)


def main_kernel(
    w_ref, owner_ref, gate_ref, x_hbm, cot_hbm,
    act_out, tok_out, sg_out, gate_out, wg_out,
    W, XS, Q, pre, PG, ACT, ggs, gs,
    SB, RSB, OWN, S, RB, T2, KB, SA, RA, SX, RX, KA, FIN, SG,
    s_loc, s_blk, s_first, r_first, s_x, r_x, s_a, r_a, s_b, r_b, r_far, s_sib, r_sib, s_cot, r_cot,
    s_sb, r_sb, credit, s_ra, r_ra, s_rb, r_rb, r_t2, s_rx, r_rx, s_fin, r_fin, s_act, r_act, s_sg, s_cmb, s_tok,
):
    e, xl, a, b, core = place()
    x = 2 * e + xl
    half = pl.ds(pl.multiple_of(core * HALF, HALF), HALF)
    other = pl.ds(pl.multiple_of((1 - core) * HALF, HALF), HALF)
    sib = device(x, b, a, 1 - core)
    along_x = {o: device(x + o, a, b, core) for o in (1, 2, 3)}
    along_a = {o: device(x, a + o, b, core) for o in (1, 3)}
    along_b = {o: device(x, a, b + o, core) for o in (1, 3)}
    next_a = {o: (a + o) % 4 for o in (1, 2, 3)} | {0: a}
    next_b = {o: (b + o) % 4 for o in (1, 2, 3)} | {0: b}
    step_a, step_b = (4 - 3 * core) * ROWS, (1 + 3 * core) * ROWS
    row_b = {o: next_b[o] * step_b for o in (0, 1, 2, 3)}
    lower, upper = pl.ds(0, 2), pl.ds(2, 2)

    def plane(j):
        ee = e + (j // 2) * (1 - 2 * e)
        flip = ((j + 1) // 2) % 2
        return ee, xl + flip * (1 - 2 * xl)

    def target(j):
        return plane(j + 1 - 2 * (j % 2))

    def away(p):
        return (2 * p[0] + p[1] - x + 4) % 4

    def block_cols(c):
        return pl.ds(pl.multiple_of(c * BLK, BLK), BLK)

    def block_of(i):
        return (i + 3 * xl) % NBLK

    def load_x(i):
        return pltpu.make_async_copy(x_hbm.at[:, block_cols(block_of(i))], SG.at[i % 2, :TOK], s_blk.at[i % 2])

    load_x(0).start()
    load_x(1).start()
    load_cot = pltpu.make_async_copy(cot_hbm.at[0, rows_at(e * CAP, CAP), :], PG.at[e], s_loc.at[0])
    load_cot.start()

    barrier = pltpu.get_barrier_semaphore()
    peers = [sib, *along_x.values(), *along_a.values(), *along_b.values()]
    for peer in peers:
        pl.semaphore_signal(barrier, inc=1, device_id=peer, device_id_type=MESH)
    pl.semaphore_wait(barrier, len(peers))

    left, right = w_ref[0, :, :HALF].astype(F32), w_ref[0, :, HALF:].astype(F32)
    FIN[1, :56] = jnp.where(core == 0, right, left)
    swap = copy_to(FIN.at[1, :56], FIN.at[0, rows_at(core * 56, 56, 8), :], s_first.at[0], r_first.at[0], sib)
    swap.start()
    FIN[0, rows_at(core * 56, 56, 8), :] = jnp.where(core == 0, left, right)
    swap.wait()

    def piece(j, o):
        ee, ll = plane(j)
        aa = next_a[o] if isinstance(o, int) else (a + o) % 4
        return W.at[core, ee, ll, aa + core * (b - aa), b + core * (aa - b)]

    def some_pieces(n):
        return W.at[0, 0, 0, 0, pl.ds(0, n)]

    W[core, e, xl, a + core * (b - a), b + core * (a - b)] = FIN[0].astype(BF16)
    mine = piece(0, 0)

    def send_a(j):
        ref = piece(j, 0)
        for s in (1, 3):
            send(ref, ref, s_a.at[j], r_a.at[j, 3 - s], along_a[s])

    def take_a(j):
        for o in (1, 3):
            arrived(some_pieces(1), r_a.at[j, o - 1])

        @pl.when(j % 2 == 0)
        def _():
            send(piece(j, 3), piece(j, 3), s_a.at[j], r_a.at[j, 1], along_a[1])

        @pl.when(j % 2 == 1)
        def _():
            send(piece(j, 1), piece(j, 1), s_a.at[j], r_a.at[j, 1], along_a[3])

    def far_a(j):
        arrived(some_pieces(1), r_a.at[j, 1])

    def send_rows(j, o, part, send_sem, recv_sem, to):
        ee, ll = plane(j)

        @pl.when(core == 0)
        def _():
            ref = W.at[core, ee, ll, part, next_b[o]]
            send(ref, ref, send_sem, recv_sem, to)

        @pl.when(core == 1)
        def _():
            ref = W.at[core, ee, ll, next_b[o], part]
            send(ref, ref, send_sem, recv_sem, to)

    def send_b(j):
        send_rows(j, 0, lower, s_b.at[j], r_b.at[j, 1, 0], along_b[1])
        send_rows(j, 0, upper, s_b.at[j], r_b.at[j, 0, 1], along_b[3])
        send_rows(j, 0, upper, s_b.at[j], r_b.at[j, 1, 1], along_b[1])
        send_rows(j, 0, lower, s_b.at[j], r_b.at[j, 0, 0], along_b[3])

    def relay_b(j):
        arrived(some_pieces(2), r_b.at[j, 1, 0])
        send_rows(j, 3, lower, s_b.at[j], r_far.at[j, 0], along_b[1])
        arrived(some_pieces(2), r_b.at[j, 0, 1])
        send_rows(j, 1, upper, s_b.at[j], r_far.at[j, 1], along_b[3])

    def rest_b(j):
        arrived(some_pieces(2), r_b.at[j, 1, 1])
        arrived(some_pieces(2), r_b.at[j, 0, 0])

    def far_b(j):
        for i in (0, 1):
            arrived(some_pieces(2), r_far.at[j, i])
        ee, ll = plane(j)
        ref = W.at[core, ee, ll]
        send(ref, ref, s_sib.at[j], r_sib.at[j], sib)

    def whole(j):
        ee, ll = plane(j)
        arrived(W.at[1 - core, ee, ll], r_sib.at[j])

    for s in (1, 3, 2):
        send(mine, mine, s_x.at[0], r_x.at[3 - s], along_x[s])
    send_a(0)

    one_hot_rows(owner_ref, Q)
    take_a(0)
    g8 = gate_ref[...].astype(F32)
    gate_row = jnp.concatenate([g8[i : i + 1] for i in range(8)], axis=1)
    gs[...] = nt(Q[...], jnp.broadcast_to(gate_row, (128, TOK)).astype(BF16)).astype(BF16)
    far_a(0)
    send_b(0)

    def dispatch(i):
        load_x(i).wait()
        for m in (0, CAP):
            XS[m : m + CAP, block_cols(block_of(i))] = nn(Q[m : m + CAP, :], SG[i % 2, :TOK]).astype(BF16)

        @pl.when(i < NBLK - 2)
        def _():
            load_x(i + 2).start()

    def start_a(j):
        arrived(some_pieces(1), r_x.at[away(plane(j)) - 1])
        send_a(j)

    loop(1, 4, start_a)
    dispatch(0)
    loop(1, 4, take_a)
    theirs_rows = rows_at((1 - e) * CAP, CAP)
    send(cot_hbm.at[0, theirs_rows, :], PG.at[e], s_cot.at[0], r_cot.at[0], along_x[2])
    far_a(1)
    send_b(1)
    dispatch(1)

    def forward(j, h):
        ee, ll = plane(j)
        cols = slice(h * HALF, (h + 1) * HALF)

        def some(i):
            rows = rows_at(i * 320, 320, 64)
            slots = XS[rows_at(ee * CAP + i * 320, 320, 64), pl.ds(pl.multiple_of(ll * PLANE, 256), PLANE)]
            part = nn(slots, W[h, ee, ll].reshape(PLANE, HALF))
            pre[rows, cols] = jnp.where(j % 2 == 0, part, pre[rows, cols] + part)

        loop(0, 2, some)

    def pointwise(k):
        def tile(i):
            rows = rows_at(i * 64, 64, 64)
            gate = gs[rows_at(k * CAP + i * 64, 64, 64), :].astype(F32)
            gate = jnp.concatenate([gate] * 4, axis=1)
            total = jnp.zeros((64, 1), F32)
            for h in (0, 1):
                cols = slice(h * HALF, (h + 1) * HALF)
                z = pre[rows, cols]
                s = 0.5 + 0.5 * jnp.tanh(0.5 * z)
                shaped = z * s
                up = PG[k, rows, cols].astype(F32)
                ACT[rows, cols] = (gate * shaped).astype(BF16)
                total += jnp.sum(up * shaped, axis=1, keepdims=True)
                PG[k, rows, cols] = (up * gate * (s * (1.0 + z * (1.0 - s)))).astype(BF16)
            ggs[rows_at(k * CAP + i * 64, 64, 64), :] = jnp.broadcast_to(total, (64, 128)).astype(BF16)

        loop(0, CAP // 64, tile)

    def theirs(j):
        ee, ll = target(j)
        def some(i):
            part = XS[rows_at(ee * CAP, CAP), pl.ds(pl.multiple_of(ll * PLANE + i * 896, 128), 896)]
            SB[rows_at(i * 896, 896, 128), :] = tn(part, PG[ee, :, other]).astype(BF16)

        loop(0, 2, some)
        send(SB, RSB.at[j % 2], s_sb.at[0], r_sb.at[j % 2], sib)

    def ours(j):
        ee, ll = target(j)
        def some(i):
            part = XS[rows_at(ee * CAP, CAP), pl.ds(pl.multiple_of(ll * PLANE + i * 896, 128), 896)]
            OWN[rows_at(i * 896, 896, 128), :] = tn(part, PG[ee, :, half])

        loop(0, 2, some)

    def first_sends(j):
        arrived(RSB.at[j % 2], r_sb.at[j % 2])
        k = j % 2

        def summed(i, o):
            rows = rows_at(row_b[o] + i * step_a, ROWS)
            return rows, OWN[rows, :] + RSB[k, rows, :].astype(F32)

        def put(o, part, dst, sem, to):
            for i in part:
                S[k, o - 1, i] = summed(i, o)[1].astype(BF16)
            part = lower if part[0] == 0 else upper
            send(S.at[k, o - 1, part], dst.at[part], s_rb.at[j], sem, to)

        put(2, (0, 1), T2.at[j], r_t2.at[j, 0], along_b[1])
        put(2, (2, 3), T2.at[j], r_t2.at[j, 1], along_b[3])
        put(1, (2, 3), RB.at[j, 1], r_rb.at[j, 1, 1], along_b[1])
        put(3, (0, 1), RB.at[j, 0], r_rb.at[j, 0, 0], along_b[3])
        for i in (0, 1, 2, 3):
            KB[k, i] = summed(i, 0)[1]
            rows, total = summed(i, 1 if i < 2 else 3)
            OWN[rows, :] = total

    def relayed_sends(j):
        k = j % 2
        for n, (part, o) in enumerate(((lower, 1), (upper, 3))):
            arrived(T2.at[j, part], r_t2.at[j, n])
            for i in (2 * n, 2 * n + 1):
                rows = rows_at(row_b[o] + i * step_a, ROWS)
                S[k, o - 1, i] = (OWN[rows, :] + T2[j, i].astype(F32)).astype(BF16)
            d = 1 - n
            send(S.at[k, o - 1, part], RB.at[j, d, part], s_rb.at[j], r_rb.at[j, d, n], along_b[o])

    def sent_b(j):
        arrived(S.at[j % 2], s_rb.at[j])

    def sent_a(j):
        arrived(SA.at[j % 2], s_ra.at[j])

    def finish_b(j):
        k = j % 2
        for d in (0, 1):
            for n, part in enumerate((lower, upper)):
                arrived(RB.at[j, d, part], r_rb.at[j, d, n])

        def total(o):
            i = next_a[o]
            return KB[k, i] + RB[j, 0, i].astype(F32) + RB[j, 1, i].astype(F32)

        @pl.when(j >= 2)
        def _():
            sent_a(j - 2)

        KA[k] = total(0)
        SA[k, 1] = total(2).astype(BF16)
        keep, go = total(1), total(3)

        @pl.when(k == 0)
        def _():
            send(SA.at[k, 1], RA.at[j, 1], s_ra.at[j], r_ra.at[j, 1], along_a[1])
            SA[k, 2] = go.astype(BF16)
            send(SA.at[k, 2], RA.at[j, 0], s_ra.at[j], r_ra.at[j, 0], along_a[3])
            FIN[1] = keep

        @pl.when(k == 1)
        def _():
            send(SA.at[k, 1], RA.at[j, 1], s_ra.at[j], r_ra.at[j, 1], along_a[3])
            SA[k, 0] = keep.astype(BF16)
            send(SA.at[k, 0], RA.at[j, 2], s_ra.at[j], r_ra.at[j, 2], along_a[1])
            FIN[1] = go

    def relay_a(j):
        k = j % 2
        arrived(RA.at[j, 1], r_ra.at[j, 1])

        @pl.when(k == 0)
        def _():
            SA[k, 0] = (FIN[1] + RA[j, 1].astype(F32)).astype(BF16)
            send(SA.at[k, 0], RA.at[j, 2], s_ra.at[j], r_ra.at[j, 2], along_a[1])

        @pl.when(k == 1)
        def _():
            SA[k, 2] = (FIN[1] + RA[j, 1].astype(F32)).astype(BF16)
            send(SA.at[k, 2], RA.at[j, 0], s_ra.at[j], r_ra.at[j, 0], along_a[3])

    def finish_a(j):
        total = KA[j % 2]
        for o in (1, 3):
            arrived(RA.at[j, o - 1], r_ra.at[j, o - 1])
            total += RA[j, o - 1].astype(F32)
        return total

    def finish_x(j):
        o = away(target(j))
        SX[o - 1] = finish_a(j).astype(BF16)
        send(SX.at[o - 1], RX.at[3 - o], s_rx.at[0], r_rx.at[3 - o], device(x + o, a, b, core))

    def slot_grad(q):
        k, n = e + (q // 4) * (1 - 2 * e), q % 4
        some = pl.ds((n % 2) * 2, 2)
        slot = q % 2

        @pl.when(q >= 2)
        def _():
            sent_sg(slot)

        def half_rows(i):
            m = rows_at(i * 320, 320, 64)
            near, far = (W[h, k, n // 2, some].reshape(896, HALF) for h in (0, 1))
            part = (nt(PG[k, m, :HALF], near) + nt(PG[k, m, HALF:], far)).astype(BF16)
            SG[0, rows_at(slot * CAP + i * 320, 320, 64), :] = part[:, :BLK]
            SG[1, rows_at(slot * CAP + i * 320, 320, 64), :384] = part[:, BLK:]

        loop(0, 2, half_rows)
        rows = rows_at(slot * CAP, CAP, 64)
        for i, (at, width) in enumerate(((0, BLK), (BLK, 384))):
            cols = pl.ds(pl.multiple_of(n * 896 + at, 128), width)
            pltpu.make_async_copy(SG.at[i, rows, :width], sg_out.at[k, :, cols], s_sg.at[slot, i]).start()

    def sent_sg(slot):
        arrived(SG.at[0, :CAP, :], s_sg.at[slot, 0])
        arrived(SG.at[1, :CAP, :384], s_sg.at[slot, 1])

    def slot_grads(first, last):
        loop(first, last, slot_grad)

    def gather_step(j):
        @pl.when(j == 3)
        def _():
            first_sends(0)
            pl.semaphore_signal(credit, inc=1, device_id=sib, device_id_type=MESH)

        relay_b(j)

        @pl.when(j == 0)
        def _():
            loop(2, 4, dispatch)

        @pl.when(j > 0)
        def _():
            whole(j - 1)
            forward(j - 1, 0)

        rest_b(j)

        @pl.when(j < 2)
        def _():
            far_a(j + 2)
            send_b(j + 2)

        @pl.when(j == 0)
        def _():
            dispatch(4)

        @pl.when(j > 0)
        def _():
            forward(j - 1, 1)

        @pl.when(j == 1)
        def _():
            loop(5, NBLK, dispatch)

        @pl.when(j == 2)
        def _():
            load_cot.wait()
            pointwise(e)
            theirs(0)
            pltpu.make_async_copy(ACT, act_out.at[0, rows_at(e * CAP, CAP), :], s_loc.at[1]).start()

        @pl.when(j == 3)
        def _():
            arrived(SB, s_sb.at[0])
            theirs(1)

        far_b(j)

        @pl.when(j == 2)
        def _():
            ours(0)

    loop(0, 4, gather_step)

    def reduce_step(j):
        @pl.when(j == 0)
        def _():
            slot_grads(0, 1)

        relayed_sends(j)

        @pl.when(j < 3)
        def _():
            ours(j + 1)

            @pl.when(j >= 1)
            def _():
                sent_b(j - 1)

            first_sends(j + 1)

        @pl.when(j == 0)
        def _():
            pl.semaphore_signal(credit, inc=1, device_id=sib, device_id_type=MESH)
            whole(3)
            forward(3, 0)
            forward(3, 1)
            arrived(PG.at[1 - e], r_cot.at[0])
            arrived(ACT, s_loc.at[1])
            pointwise(1 - e)
            send(ACT, act_out.at[0, rows_at(e * CAP, CAP), :], s_act.at[0], r_act.at[0], along_x[2])

        @pl.when(j < 2)
        def _():
            arrived(SB, s_sb.at[0])
            pl.semaphore_wait(credit, 1)
            theirs(j + 2)

        @pl.when(j >= 1)
        def _():
            relay_a(j - 1)

        @pl.when(j == 2)
        def _():
            finish_x(0)

        @pl.when(j == 3)
        def _():
            FIN[0] = finish_a(1)

        @pl.when(j >= 1)
        def _():
            slot_grads(2 * j, 2 * j + 2)

        @pl.when(j == 0)
        def _():
            slot_grads(1, 2)

        finish_b(j)

    loop(0, 4, reduce_step)
    sent_sg(0)
    sent_sg(1)

    def early(c):
        for k in (0, 1):
            pltpu.make_async_copy(
                sg_out.at[k, :, block_cols(c)], SG.at[c % 2, k * CAP : (k + 1) * CAP], s_cmb.at[c % 2]
            ).start()

    def combine(c):
        arrived(SG.at[c % 2], s_cmb.at[c % 2])

        @pl.when(c >= 2)
        def _():
            arrived(RSB.at[c % 2, :TOK], s_tok.at[c % 2])

        def some(i):
            m = pl.ds(pl.multiple_of(i * 512, 512), 512)
            RSB[c % 2, m] = tn(Q[:, m], SG[c % 2]).astype(BF16)

        loop(0, 2, some)
        pltpu.make_async_copy(RSB.at[c % 2, :TOK], tok_out.at[:, block_cols(c)], s_tok.at[c % 2]).start()

        @pl.when(c + 2 < EARLY)
        def _():
            early(c + 2)

    early(0)
    early(1)
    finish_x(2)
    combine(0)
    relay_a(3)
    loop(1, EARLY, combine)
    gg = ggs[...].astype(F32).T[:8].astype(BF16)
    row = nn(gg, Q[...])
    gate_out[...] = jnp.concatenate([row[:1, i * 128 : (i + 1) * 128] for i in range(8)], axis=0)
    finish_x(3)
    total = FIN[0]
    for o in (1, 2, 3):
        arrived(RX.at[o - 1], r_rx.at[o - 1])
        total += RX[o - 1].astype(F32)
    FIN[0] = total
    away_rows = rows_at((1 - core) * 56, 56, 8)
    kept_rows = rows_at(core * 56, 56, 8)
    last = copy_to(FIN.at[0, away_rows, :], FIN.at[2, away_rows, :], s_fin.at[0], r_fin.at[0], sib)
    last.start()
    last.wait_send()
    arrived(FIN.at[2, kept_rows, :], r_fin.at[0])
    kept, came = FIN[0, kept_rows, :], FIN[2, kept_rows, :]
    wg_out[0, :, :HALF] = jnp.where(core == 0, kept, came)
    wg_out[0, :, HALF:] = jnp.where(core == 0, came, kept)

    arrived(some_pieces(3), s_x.at[0])
    arrived(SX, s_rx.at[0])
    arrived(cot_hbm.at[0, theirs_rows, :], s_cot.at[0])
    arrived(ACT, s_act.at[0])
    arrived(SB, s_sb.at[0])
    arrived(act_out.at[0, theirs_rows, :], r_act.at[0])
    for i in (0, 1):
        arrived(RSB.at[i, :TOK], s_tok.at[i])

    def drain(j):
        arrived(some_pieces(3), s_a.at[j])
        arrived(W.at[0, 0, 0, pl.ds(0, 3)], s_b.at[j])
        arrived(W.at[0, 0, 0], s_sib.at[j])

        @pl.when(j >= 2)
        def _():
            sent_a(j)
            sent_b(j)

    loop(0, 4, drain)


def combine_kernel(
    owner_ref, gate_ref, sg_hbm, tok_hbm, act_hbm, wg_hbm,
    gate_out, tok_out, act_out, wg_out,
    Q, SG, TB, TV, AV, GV, s_sg, s_tok, s_in, s_out,
):
    def cols(c):
        return pl.ds(pl.multiple_of(c * BLK, BLK), BLK)

    def load(c):
        return [
            pltpu.make_async_copy(
                sg_hbm.at[k, :, cols(c)], SG.at[c % 2, k * CAP : (k + 1) * CAP], s_sg.at[c % 2, k]
            )
            for k in (0, 1)
        ]

    moves = [
        (act_hbm, AV, act_out),
        (tok_hbm, TV, tok_out.at[:, : EARLY * BLK]),
        (wg_hbm, GV, wg_out),
    ]
    moves = [
        (pltpu.make_async_copy(p, v, s_in.at[i]), pltpu.make_async_copy(v, q, s_out.at[i]))
        for i, (p, v, q) in enumerate(moves)
    ]
    for c in (EARLY, EARLY + 1):
        for k in load(c):
            k.start()
    for k, _ in moves:
        k.start()
    one_hot_rows(owner_ref, Q)
    gate_out[...] = gate_ref[...].astype(BF16)

    def combine(c):
        for k in load(c):
            k.wait()

        @pl.when(c >= EARLY + 2)
        def _():
            arrived(TB.at[c % 2], s_tok.at[c % 2])

        TB[c % 2] = tn(Q[...], SG[c % 2]).astype(BF16)
        pltpu.make_async_copy(TB.at[c % 2], tok_out.at[:, cols(c)], s_tok.at[c % 2]).start()

        @pl.when(c + 2 < NBLK)
        def _():
            for k in load(c + 2):
                k.start()

    loop(EARLY, EARLY + 1, combine)
    for k, m in moves:
        k.wait()
        m.start()
    loop(EARLY + 1, NBLK, combine)
    for i in (0, 1):
        arrived(TB.at[i], s_tok.at[i])
    for _, m in moves:
        m.wait()


def body(tokens, assignment, gate, weight, cotangent):
    ANY, VMEM = pl.BlockSpec(memory_space=pl.ANY), pl.BlockSpec(memory_space=pltpu.VMEM)
    DMA = pltpu.SemaphoreType.DMA
    shape = jax.ShapeDtypeStruct
    owner = assignment.reshape(1, TOK)
    act, tok, sg, grad_gate, grad_weight = pl.pallas_call(
        main_kernel,
        out_shape=(
            shape((1, 2 * CAP, F), BF16),
            shape((TOK, EARLY * BLK), BF16),
            shape((2, CAP, D), BF16),
            shape((8, 128), F32),
            shape((1, 56, F), F32),
        ),
        in_specs=[VMEM, VMEM, VMEM, ANY, ANY],
        out_specs=(ANY, ANY, ANY, VMEM, VMEM),
        scratch_shapes=[
            pltpu.VMEM((2, 2, 2, 4, 4, ROWS, HALF), BF16),
            pltpu.VMEM((2 * CAP, D), BF16),
            pltpu.VMEM((2 * CAP, TOK), BF16),
            pltpu.VMEM((CAP, F), F32),
            pltpu.VMEM((2, CAP, F), BF16),
            pltpu.VMEM((CAP, F), BF16),
            pltpu.VMEM((2 * CAP, 128), BF16),
            pltpu.VMEM((2 * CAP, 128), BF16),
            pltpu.VMEM((PLANE, HALF), BF16),
            pltpu.VMEM((2, PLANE, HALF), BF16),
            pltpu.VMEM((PLANE, HALF), F32),
            pltpu.VMEM((2, 3, 4, ROWS, HALF), BF16),
            pltpu.VMEM((4, 2, 4, ROWS, HALF), BF16),
            pltpu.VMEM((4, 4, ROWS, HALF), BF16),
            pltpu.VMEM((2, 4, ROWS, HALF), F32),
            pltpu.VMEM((2, 3, ROWS, HALF), BF16),
            pltpu.VMEM((4, 3, ROWS, HALF), BF16),
            pltpu.VMEM((3, ROWS, HALF), BF16),
            pltpu.VMEM((3, ROWS, HALF), BF16),
            pltpu.VMEM((2, ROWS, HALF), F32),
            pltpu.VMEM((3, ROWS, HALF), F32),
            pltpu.VMEM((2, 2 * CAP, BLK), BF16),
            DMA((2,)), DMA((2,)), DMA((1,)), DMA((1,)), DMA((1,)), DMA((3,)), DMA((4,)), DMA((4, 3)),
            DMA((4,)), DMA((4, 2, 2)), DMA((4, 2)), DMA((4,)), DMA((4,)), DMA((1,)), DMA((1,)),
            DMA((1,)), DMA((2,)), pltpu.SemaphoreType.REGULAR, DMA((4,)), DMA((4, 3)),
            DMA((4,)), DMA((4, 2, 2)), DMA((4, 2)), DMA((1,)), DMA((3,)), DMA((1,)), DMA((1,)), DMA((1,)), DMA((1,)),
            DMA((2, 2)), DMA((2,)), DMA((2,)),
        ],
        compiler_params=pltpu.CompilerParams(collective_id=1, has_side_effects=True, vmem_limit_bytes=62 * 2**20),
        name="gather_and_reduce",
    )(weight, owner, gate.reshape(8, 128), tokens, cotangent)
    grad_gate, grad_tokens, activated, grad_weight = pl.pallas_call(
        combine_kernel,
        out_shape=(
            shape((8, 128), BF16),
            shape((TOK, D), BF16),
            shape((1, 2 * CAP, F), BF16),
            shape((1, 56, F), F32),
        ),
        in_specs=[VMEM, VMEM, ANY, ANY, ANY, ANY],
        out_specs=(VMEM, ANY, ANY, ANY),
        scratch_shapes=[
            pltpu.VMEM((2 * CAP, TOK), BF16),
            pltpu.VMEM((2, 2 * CAP, BLK), BF16),
            pltpu.VMEM((2, TOK, BLK), BF16),
            pltpu.VMEM((TOK, EARLY * BLK), BF16),
            pltpu.VMEM((1, 2 * CAP, F), BF16),
            pltpu.VMEM((1, 56, F), F32),
            DMA((2, 2)), DMA((2,)), DMA((3,)), DMA((3,)),
        ],
        compiler_params=pltpu.CompilerParams(vmem_limit_bytes=60 * 2**20),
        name="combine_tokens",
    )(owner, grad_gate, sg, tok, act, grad_weight)
    return activated, grad_tokens, grad_gate.reshape(TOK), grad_weight


def solution(mesh):
    placed = (
        P(("dp", "expert"), None),
        P(("dp", "expert"), None),
        P(("dp", "expert")),
        P("expert", "dp", None),
        P("expert", "dp", None),
    )
    return jax.shard_map(
        body,
        mesh=mesh,
        in_specs=placed,
        out_specs=(
            P("expert", "dp", None),
            P(("dp", "expert"), None),
            P(("dp", "expert")),
            P("expert", "dp", None),
        ),
        check_vma=False,
    )
```

time: 144 us -> 142 us (0.986)
  Pallas kernels: 143 us -> 141 us
    pallas_call x1, Pallas kernels: 133 us -> 130 us  [body(): pl.pallas_call(main_kernel, out_shape=(shape((1, 2 * CAP, F), BF16), shap...]
where the time goes in v1:
time: 142 us
  Pallas kernels  141 us (99%)
    pallas_call x1, Pallas kernels, body(): pl.pallas_call(main_kernel, out_shape=(shape((1, 2 * CAP, F), BF16), shap...  130 us
    pallas_call x1, Pallas kernels, body(): pl.pallas_call(combine_kernel, out_shape=(shape((8, 128), BF16), shape((T...  10.7 us

profile of v1, /device:TPU:1, one launch (start us, length us, event | category | flops | bytes accessed | tf_op | source)
XLA Modules:
  0.0 141.7 jit_solution(9132938054334710481)
XLA Ops:
  0.6 130.3 %gather_and_reduce.1 = (bf16[1,1280,1024]{2,1,0:T(8,128)(2,1)}, bf16[1024,1536]{1,0:T(8,128)(2,1)}, bf16[2,640,3584]{2,1,0:T(8,128)(2,1)}, f32[8,128]{1,0:T(8,128)}, f32[1,56,1024]{2,1,0:T(8,128)}) custom-call(bf16[1,56,1024]{2,1,0:T(8,128)(2,1)} %w_ref.1, s32[1,1024]{1,0:T(1,128)} %bitcast.3, bf16[8,128]{1,0:T(8,128)(2,1)} %bitcast.5, ...), custom_call_target="tpu_custom_call" | custom-call | tf_op jit(solution)/shard_map/gather_and_reduce/pallas_call | solution.py:683
  130.9 10.7 %combine_tokens.1 = (bf16[8,128]{1,0:T(8,128)(2,1)}, bf16[1024,3584]{1,0:T(8,128)(2,1)}, bf16[1,1280,1024]{2,1,0:T(8,128)(2,1)}, f32[1,56,1024]{2,1,0:T(8,128)}) custom-call(s32[1,1024]{1,0:T(1,128)} %bitcast.4, f32[8,128]{1,0:T(8,128)} %get-tuple-element.13.gate_ref, bf16[2,640,3584]{2,1,0:T(8,128)(2,1)} %get-tuple-element.14.sg_hbm, ...), custom_call_target="tpu_custom_call" | custom-call | tf_op jit(solution)/shard_map/combine_tokens/pallas_call | solution.py:726

commit v2 on v1

--- a/solution.py
+++ b/solution.py
@@ -257,14 +257,9 @@
     def forward(j, h):
         ee, ll = plane(j)
         cols = slice(h * HALF, (h + 1) * HALF)
-
-        def some(i):
-            rows = rows_at(i * 320, 320, 64)
-            slots = XS[rows_at(ee * CAP + i * 320, 320, 64), pl.ds(pl.multiple_of(ll * PLANE, 256), PLANE)]
-            part = nn(slots, W[h, ee, ll].reshape(PLANE, HALF))
-            pre[rows, cols] = jnp.where(j % 2 == 0, part, pre[rows, cols] + part)
-
-        loop(0, 2, some)
+        slots = XS[rows_at(ee * CAP, CAP), pl.ds(pl.multiple_of(ll * PLANE, 256), PLANE)]
+        part = nn(slots, W[h, ee, ll].reshape(PLANE, HALF))
+        pre[:, cols] = jnp.where(j % 2 == 0, part, pre[:, cols] + part)
 
     def pointwise(k):
         def tile(i):
@@ -557,11 +552,7 @@
         def _():
             arrived(RSB.at[c % 2, :TOK], s_tok.at[c % 2])
 
-        def some(i):
-            m = pl.ds(pl.multiple_of(i * 512, 512), 512)
-            RSB[c % 2, m] = tn(Q[:, m], SG[c % 2]).astype(BF16)
-
-        loop(0, 2, some)
+        RSB[c % 2, :TOK] = tn(Q[...], SG[c % 2]).astype(BF16)
         pltpu.make_async_copy(RSB.at[c % 2, :TOK], tok_out.at[:, block_cols(c)], s_tok.at[c % 2]).start()
 
         @pl.when(c + 2 < EARLY)

time: 142 us -> 140 us (0.986)
  Pallas kernels: 141 us -> 139 us
    pallas_call x1, Pallas kernels: 130 us -> 128 us  [body(): pl.pallas_call(main_kernel, out_shape=(shape((1, 2 * CAP, F), BF16), shap...]
where the time goes in v2:
time: 140 us
  Pallas kernels  139 us (99%)
    pallas_call x1, Pallas kernels, body(): pl.pallas_call(main_kernel, out_shape=(shape((1, 2 * CAP, F), BF16), shap...  128 us
    pallas_call x1, Pallas kernels, body(): pl.pallas_call(combine_kernel, out_shape=(shape((8, 128), BF16), shape((T...  10.7 us

profile of v2, /device:TPU:1, one launch (start us, length us, event | category | flops | bytes accessed | tf_op | source)
XLA Modules:
  0.0 139.6 jit_solution(18002341261264228052)
XLA Ops:
  0.6 128.2 %gather_and_reduce.1 = (bf16[1,1280,1024]{2,1,0:T(8,128)(2,1)}, bf16[1024,1536]{1,0:T(8,128)(2,1)}, bf16[2,640,3584]{2,1,0:T(8,128)(2,1)}, f32[8,128]{1,0:T(8,128)}, f32[1,56,1024]{2,1,0:T(8,128)}) custom-call(bf16[1,56,1024]{2,1,0:T(8,128)(2,1)} %w_ref.1, s32[1,1024]{1,0:T(1,128)} %bitcast.3, bf16[8,128]{1,0:T(8,128)(2,1)} %bitcast.5, ...), custom_call_target="tpu_custom_call" | custom-call | tf_op jit(solution)/shard_map/gather_and_reduce/pallas_call | solution.py:674
  128.8 10.7 %combine_tokens.1 = (bf16[8,128]{1,0:T(8,128)(2,1)}, bf16[1024,3584]{1,0:T(8,128)(2,1)}, bf16[1,1280,1024]{2,1,0:T(8,128)(2,1)}, f32[1,56,1024]{2,1,0:T(8,128)}) custom-call(s32[1,1024]{1,0:T(1,128)} %bitcast.4, f32[8,128]{1,0:T(8,128)} %get-tuple-element.13.gate_ref, bf16[2,640,3584]{2,1,0:T(8,128)(2,1)} %get-tuple-element.14.sg_hbm, ...), custom_call_target="tpu_custom_call" | custom-call | tf_op jit(solution)/shard_map/combine_tokens/pallas_call | solution.py:717
